TPU v7x, 128 devices: a whole 4x4x4 slice. The times are simulated.
128 devices in a mesh: seq: 2 (over y_hi), dp: 64 (over y_lo, z, x, core).
Axes of the slice: x: 4, y: 4 (y_hi: 2, y_lo: 2; y = y_hi * 2 + y_lo), z: 4, core: 2. Of those that a mesh axis runs over, the one named last changes fastest.
Arguments:
- tokens: bfloat16 [65536, 768], P(('seq', 'dp')), may hold values from -6 to 6
- input_weight: bfloat16 [768, 2304], replicated, may hold values from -0.21875 to 0.21875
- query_bias: float32 [768], replicated, may hold values from -3 to 3
- value_bias: float32 [768], replicated, may hold values from -1.2 to 1.2
- out_weight: bfloat16 [768, 768], replicated, may hold values from -1.75 to 1.75
- out_bias: float32 [768], replicated, may hold values from -2 to 2
- first_gain: float32 [768], replicated, may hold values from 0.5 to 1.5
- first_shift: float32 [768], replicated, may hold values from -2 to 2
- second_gain: float32 [768], replicated, may hold values from 0.5 to 1.5
- second_shift: float32 [768], replicated, may hold values from -2 to 2
- up_weight: bfloat16 [768, 3072], replicated, may hold values from -0.21875 to 0.21875
- up_bias: float32 [3072], replicated, may hold values from -2 to 2
- down_weight: bfloat16 [3072, 768], replicated, may hold values from -0.109375 to 0.109375
- down_bias: float32 [768], replicated, may hold values from -2 to 2
- cotangent: bfloat16 [65536, 768], P(('seq', 'dp')), may hold values from -6 to 6
- row_counts: int32 [64, 2], P('dp'), may hold values from 128 to 512, as said below
- image_lengths: int32 [64, 4], P('dp'), may hold values from 1 to 1021, as said below
Outputs:
- layer_out: bfloat16 [65536, 768], P(('seq', 'dp'))
- grad_tokens: bfloat16 [65536, 768], P(('seq', 'dp'))
- grad_input_weight: float32 [768, 2304], P('dp')
- grad_query_bias: float32 [768], P('dp')
- grad_value_bias: float32 [768], P('dp')
- grad_out_weight: float32 [768, 768], P('dp')
- grad_out_bias: float32 [768], P('dp')
- grad_first_gain: float32 [768], P('dp')
- grad_first_shift: float32 [768], P('dp')
- grad_second_gain: float32 [768], P('dp')
- grad_second_shift: float32 [768], P('dp')
- grad_up_weight: float32 [768, 3072], P('dp')
- grad_up_bias: float32 [3072], P('dp')
- grad_down_weight: float32 [3072, 768], P('dp')
- grad_down_bias: float32 [768], P('dp')
Inputs may be any that keep to these rules, and one draw needn't show every extreme that they name: row_counts[n, s] is the number of used rows of part s of sequence n; in every sequence one of the two counts is exactly 512. `image_lengths`: the 4 lengths of a sequence sum to its two row counts together; the third image holds the last used row of part 0 and the first row of part 1.
All inputs are finite; a program needn't handle non-finite values.
Results may differ from a plain program's by a relative error of at most 0.015.
Values may be sent and summed in bfloat16 or wider, within the bound.
A program may use at most 256 MiB of HBM per device.

v0:
```python
import math

import jax
import jax.numpy as jnp
from jax import lax
from jax.sharding import PartitionSpec as P

HEADS = 12
HD = 64


EPS = 1e-06
MASKED = -1e30


def passed_along(value, axis, steps):
    count = lax.axis_size(axis)
    pairs = [(source, (source + steps) % count) for source in range(count)]
    return lax.ppermute(value, axis, pairs)


def norm_rows(row_block, norm_gain, norm_shift):
    row_mean = jnp.mean(row_block, axis=-1, keepdims=True)
    centred = row_block - row_mean
    spread = jnp.mean(centred * centred, axis=-1, keepdims=True)
    return centred * lax.rsqrt(spread + EPS) * norm_gain + norm_shift


def gelu_exact(pre_act):
    return jax.nn.gelu(pre_act, approximate=False)


def labels(counts, lengths, part_index, slot_count):
    places = jnp.arange(slot_count, dtype=jnp.int32)
    image_ends = jnp.cumsum(lengths)
    shifted = places + part_index * counts[0]
    image_index = jnp.sum((image_ends[None, :] <= shifted[:, None]).astype(jnp.int32), axis=1)
    owned_rows = jnp.where(part_index == 0, counts[0], counts[1])
    used_rows = places < owned_rows
    image_ids = jnp.where(
        used_rows, image_index, lengths.shape[0] + part_index * slot_count + places
    )
    return (image_ids, used_rows)


def split_heads(row_block):
    return row_block.reshape(row_block.shape[0], HEADS, HD)


def inner_rows(left, right):
    return lax.dot_general(
        left, right, (((0,), (0,)), ((), ())), preferred_element_type=jnp.float32
    )


def back_dot(left, right):
    return lax.dot_general(
        left, right, (((1,), (1,)), ((), ())), preferred_element_type=jnp.float32
    )


def scores_of(queries, key_rows, same_image, score_scale):
    raw_scores = (
        jnp.einsum(
            "qhd,khd->hqk",
            split_heads(queries),
            split_heads(key_rows),
            preferred_element_type=jnp.float32,
        )
        * score_scale
    )
    return jnp.where(same_image[None], raw_scores, MASKED)


def body(
    tokens,
    input_weight,
    query_bias,
    value_bias,
    out_weight,
    out_bias,
    first_gain,
    first_shift,
    second_gain,
    second_shift,
    up_weight,
    up_bias,
    down_weight,
    down_bias,
    cotangent,
    row_counts,
    image_lengths,
):
    local_rows = tokens.shape[0]
    model_width = tokens.shape[1]
    score_scale = 1.0 / math.sqrt(HD)
    part_index = lax.axis_index("seq")
    counts = row_counts[0]
    lengths = image_lengths[0]
    own_ids, own_used = labels(counts, lengths, part_index, local_rows)
    far_ids, far_used = labels(counts, lengths, 1 - part_index, local_rows)
    near_mask = own_ids[:, None] == own_ids[None, :]
    far_mask = own_ids[:, None] == far_ids[None, :]
    used_rows = own_used.astype(jnp.float32)[:, None]
    inputs = tokens.astype(jnp.float32)

    def attention_inputs(row_block):
        normed = norm_rows(row_block, first_gain, first_shift).astype(jnp.bfloat16)
        projected = jnp.dot(normed, input_weight, preferred_element_type=jnp.float32)
        queries = (projected[:, 0:model_width] + query_bias).astype(jnp.bfloat16)
        near_keys = projected[:, model_width : 2 * model_width].astype(jnp.bfloat16)
        near_values = (projected[:, 2 * model_width : 3 * model_width] + value_bias).astype(
            jnp.bfloat16
        )
        return (normed, queries, near_keys, near_values)

    def attended_rows(near_probs, far_probs, near_values, far_values):
        joined_heads = jnp.einsum(
            "hqk,khd->qhd",
            near_probs.astype(jnp.bfloat16),
            split_heads(near_values),
            preferred_element_type=jnp.float32,
        )
        joined_heads = joined_heads + jnp.einsum(
            "hqk,khd->qhd",
            far_probs.astype(jnp.bfloat16),
            split_heads(far_values),
            preferred_element_type=jnp.float32,
        )
        return joined_heads.reshape(local_rows, model_width).astype(jnp.bfloat16)

    def mlp_inputs(residual):
        second = norm_rows(residual, second_gain, second_shift).astype(jnp.bfloat16)
        hidden = jnp.dot(second, up_weight, preferred_element_type=jnp.float32) + up_bias
        active = gelu_exact(hidden).astype(jnp.bfloat16)
        return (second, hidden, active)

    normed, queries, near_keys, near_values = attention_inputs(inputs)
    far_keys, far_values = passed_along((near_keys, near_values), "seq", 1)
    near_scores = scores_of(queries, near_keys, near_mask, score_scale)
    far_scores = scores_of(queries, far_keys, far_mask, score_scale)
    top_score = jnp.maximum(jnp.max(near_scores, axis=-1), jnp.max(far_scores, axis=-1))
    exp_total = jnp.sum(jnp.exp(near_scores - top_score[..., None]), axis=-1) + jnp.sum(
        jnp.exp(far_scores - top_score[..., None]), axis=-1
    )
    log_total = top_score + jnp.log(exp_total)
    near_probs = jnp.exp(near_scores - log_total[..., None])
    far_probs = jnp.exp(far_scores - log_total[..., None])
    attended = attended_rows(near_probs, far_probs, near_values, far_values)
    residual = inputs + jnp.dot(attended, out_weight, preferred_element_type=jnp.float32) + out_bias
    second, hidden, active = mlp_inputs(residual)
    result = residual + jnp.dot(active, down_weight, preferred_element_type=jnp.float32) + down_bias
    layer_out = (result * used_rows).astype(jnp.bfloat16)
    inputs_again, residual_again, log_again = lax.optimization_barrier(
        (inputs, residual, log_total)
    )
    normed, queries, near_keys, near_values = attention_inputs(inputs_again)
    far_keys, far_values = passed_along((near_keys, near_values), "seq", 1)
    near_probs = jnp.exp(
        scores_of(queries, near_keys, near_mask, score_scale) - log_again[..., None]
    )
    far_probs = jnp.exp(scores_of(queries, far_keys, far_mask, score_scale) - log_again[..., None])
    attended = attended_rows(near_probs, far_probs, near_values, far_values)
    second, hidden, active = mlp_inputs(residual_again)
    grad_out = cotangent.astype(jnp.float32) * used_rows
    grad_low = grad_out.astype(jnp.bfloat16)
    down_weight_grad = inner_rows(active, grad_low)
    down_bias_grad = jnp.sum(grad_out, axis=0)
    active_grad = back_dot(grad_low, down_weight)
    gelu_pull = jax.vjp(gelu_exact, hidden)[1]
    hidden_grad = gelu_pull(active_grad)[0].astype(jnp.bfloat16)
    up_weight_grad = inner_rows(second, hidden_grad)
    up_bias_grad = jnp.sum(hidden_grad.astype(jnp.float32), axis=0)
    second_grad = back_dot(hidden_grad, up_weight)
    second_pull = jax.vjp(norm_rows, residual, second_gain, second_shift)[1]
    through_second, second_gain_grad, second_shift_grad = second_pull(second_grad)
    residual_grad = grad_out + through_second
    feed_terms = (
        up_weight_grad,
        up_bias_grad,
        down_weight_grad,
        down_bias_grad,
        second_gain_grad,
        second_shift_grad,
    )
    feed_whole = (
        lax.psum(feed_terms[0].astype(jnp.bfloat16), "seq").astype(jnp.float32),
        lax.psum(feed_terms[1].astype(jnp.bfloat16), "seq").astype(jnp.float32),
        lax.psum(feed_terms[2].astype(jnp.bfloat16), "seq").astype(jnp.float32),
        lax.psum(feed_terms[3].astype(jnp.bfloat16), "seq").astype(jnp.float32),
        lax.psum(feed_terms[4].astype(jnp.bfloat16), "seq").astype(jnp.float32),
        lax.psum(feed_terms[5].astype(jnp.bfloat16), "seq").astype(jnp.float32),
    )
    feed_share = (
        lax.psum_scatter(feed_whole[0], "dp", scatter_dimension=0, tiled=True),
        lax.psum_scatter(feed_whole[1], "dp", scatter_dimension=0, tiled=True),
        lax.psum_scatter(feed_whole[2], "dp", scatter_dimension=0, tiled=True),
        lax.psum_scatter(feed_whole[3], "dp", scatter_dimension=0, tiled=True),
        lax.psum_scatter(feed_whole[4], "dp", scatter_dimension=0, tiled=True),
        lax.psum_scatter(feed_whole[5], "dp", scatter_dimension=0, tiled=True),
    )
    branch_grad = residual_grad.astype(jnp.bfloat16)
    out_weight_grad = inner_rows(attended, branch_grad)
    out_bias_grad = jnp.sum(branch_grad.astype(jnp.float32), axis=0)
    heads_grad = split_heads(back_dot(branch_grad, out_weight).astype(jnp.bfloat16))
    near_values_grad = jnp.einsum(
        "hqk,qhd->khd",
        near_probs.astype(jnp.bfloat16),
        heads_grad,
        preferred_element_type=jnp.float32,
    )
    far_values_grad = jnp.einsum(
        "hqk,qhd->khd",
        far_probs.astype(jnp.bfloat16),
        heads_grad,
        preferred_element_type=jnp.float32,
    )
    near_dprobs = jnp.einsum(
        "qhd,khd->hqk", heads_grad, split_heads(near_values), preferred_element_type=jnp.float32
    )
    far_dprobs = jnp.einsum(
        "qhd,khd->hqk", heads_grad, split_heads(far_values), preferred_element_type=jnp.float32
    )
    delta_rows = jnp.sum(near_probs * near_dprobs, axis=-1) + jnp.sum(
        far_probs * far_dprobs, axis=-1
    )
    near_dscores = (near_probs * (near_dprobs - delta_rows[..., None])).astype(jnp.bfloat16)
    far_dscores = (far_probs * (far_dprobs - delta_rows[..., None])).astype(jnp.bfloat16)
    query_grad = jnp.einsum(
        "hqk,khd->qhd", near_dscores, split_heads(near_keys), preferred_element_type=jnp.float32
    )
    query_grad = (
        query_grad
        + jnp.einsum(
            "hqk,khd->qhd", far_dscores, split_heads(far_keys), preferred_element_type=jnp.float32
        )
    ) * score_scale
    near_keys_grad = (
        jnp.einsum(
            "hqk,qhd->khd", near_dscores, split_heads(queries), preferred_element_type=jnp.float32
        )
        * score_scale
    )
    far_keys_grad = (
        jnp.einsum(
            "hqk,qhd->khd", far_dscores, split_heads(queries), preferred_element_type=jnp.float32
        )
        * score_scale
    )
    sent_keys = far_keys_grad.reshape(local_rows, model_width)
    sent_values = far_values_grad.reshape(local_rows, model_width)
    back_keys, back_values = (
        passed_along(sent_keys.astype(jnp.bfloat16), "seq", 1).astype(sent_keys.dtype),
        passed_along(sent_values.astype(jnp.bfloat16), "seq", 1).astype(sent_values.dtype),
    )
    keys_total = (near_keys_grad.reshape(local_rows, model_width) + back_keys).astype(jnp.bfloat16)
    values_total = (near_values_grad.reshape(local_rows, model_width) + back_values).astype(
        jnp.bfloat16
    )
    query_low = query_grad.reshape(local_rows, model_width).astype(jnp.bfloat16)
    joined = jnp.concatenate([query_low, keys_total, values_total], axis=1)
    input_weight_grad = inner_rows(normed, joined)
    query_bias_grad = jnp.sum(query_low.astype(jnp.float32), axis=0)
    value_bias_grad = jnp.sum(values_total.astype(jnp.float32), axis=0)
    first_grad = back_dot(joined, input_weight)
    first_pull = jax.vjp(norm_rows, inputs, first_gain, first_shift)[1]
    through_first, first_gain_grad, first_shift_grad = first_pull(first_grad)
    grad_tokens = (residual_grad + through_first).astype(jnp.bfloat16)
    attend_terms = (
        input_weight_grad,
        query_bias_grad,
        value_bias_grad,
        out_weight_grad,
        out_bias_grad,
        first_gain_grad,
        first_shift_grad,
    )
    attend_whole = (
        lax.psum(attend_terms[0].astype(jnp.bfloat16), "seq").astype(jnp.float32),
        lax.psum(attend_terms[1].astype(jnp.bfloat16), "seq").astype(jnp.float32),
        lax.psum(attend_terms[2].astype(jnp.bfloat16), "seq").astype(jnp.float32),
        lax.psum(attend_terms[3].astype(jnp.bfloat16), "seq").astype(jnp.float32),
        lax.psum(attend_terms[4].astype(jnp.bfloat16), "seq").astype(jnp.float32),
        lax.psum(attend_terms[5].astype(jnp.bfloat16), "seq").astype(jnp.float32),
        lax.psum(attend_terms[6].astype(jnp.bfloat16), "seq").astype(jnp.float32),
    )
    attend_share = (
        lax.psum_scatter(attend_whole[0], "dp", scatter_dimension=0, tiled=True),
        lax.psum_scatter(attend_whole[1], "dp", scatter_dimension=0, tiled=True),
        lax.psum_scatter(attend_whole[2], "dp", scatter_dimension=0, tiled=True),
        lax.psum_scatter(attend_whole[3], "dp", scatter_dimension=0, tiled=True),
        lax.psum_scatter(attend_whole[4], "dp", scatter_dimension=0, tiled=True),
        lax.psum_scatter(attend_whole[5], "dp", scatter_dimension=0, tiled=True),
        lax.psum_scatter(attend_whole[6], "dp", scatter_dimension=0, tiled=True),
    )
    return (
        layer_out,
        grad_tokens,
        attend_share[0],
        attend_share[1],
        attend_share[2],
        attend_share[3],
        attend_share[4],
        attend_share[5],
        attend_share[6],
        feed_share[4],
        feed_share[5],
        feed_share[0],
        feed_share[1],
        feed_share[2],
        feed_share[3],
    )


def solution(mesh):
    placed = (
        P(("seq", "dp"), None),
        P(),
        P(),
        P(),
        P(),
        P(),
        P(),
        P(),
        P(),
        P(),
        P(),
        P(),
        P(),
        P(),
        P(("seq", "dp"), None),
        P("dp", None),
        P("dp", None),
    )
    return jax.shard_map(
        body,
        mesh=mesh,
        in_specs=placed,
        out_specs=(
            P(("seq", "dp"), None),
            P(("seq", "dp"), None),
            P("dp", None),
            P("dp"),
            P("dp"),
            P("dp", None),
            P("dp"),
            P("dp"),
            P("dp"),
            P("dp"),
            P("dp"),
            P("dp", None),
            P("dp"),
            P("dp", None),
            P("dp"),
        ),
        check_vma=False,
    )
```

profile of v0, /device:TPU:0, one launch (start us, length us, event | category | flops | bytes accessed | tf_op | source)
XLA Modules:
  0.0 1453.1 jit_solution(8096385365127807165)
XLA Ops:
  35.3 8.7 fusion.3
  44.0 9.6 collective-permute-done
  55.9 3.6 fusion.4
  62.7 5.6 exponential_reduce_fusion
  68.3 4.0 fusion.22
  74.7 8.6 add_convert_fusion.6
  89.3 3.5 fusion.114
  116.0 18.3 %fusion.10 = (f32[512,3072]{1,0:T(8,128)S(1)}, f32[512,3072]{1,0:T(8,128)S(1)}) fusion(f32[3072]{0:T(1024)S(1)} %copy-done.55, bf16[768,3072]{1,0:T(8,128)(2,1)} %param.27, f32[512,768]{1,0:T(8,128)} %get-tuple-element.18, f32[512]{0:T(512)} %add_rsqrt_fusion.1, f32[512]{0:T(512)} %copy-done.80, f32[768]{0:T(1024)} %param.26, f32[768]{0:T(1024)} %param.25), kind=kOutput, calls=%fused_computation.21 | convolution fusion | flops 2516975616 | bytes 18896896 | tf_op jit(solution)/shard_map/dot_general | solution.py:134
  134.3 13.6 fusion.126
  148.0 6.8 convolution_convert_fusion.1
  154.9 5.9 multiply_reduce_fusion.2
  171.8 4.1 fusion.60
  178.2 4.3 fusion.62
  182.6 6.4 fusion.128
  189.0 8.3 convolution_convert_fusion
  203.0 4.5 convolution_convert_fusion.5
  213.3 9.4 add_convert_fusion.1
  222.7 21.2 %multiply_reduce_fusion = (f32[12,512]{1,0:T(8,128)}, f32[12,512]{1,0:T(8,128)}, f32[12,512,512]{1,2,0:T(8,128)}) fusion(f32[12,512,512]{1,2,0:T(8,128)} %copy-done.2, f32[12,512]{1,0:T(8,128)} %copy-done.36, pred[512,512]{0,1:T(8,128)(4,1)} %get-tuple-element.76, f32[12,512,512]{1,2,0:T(8,128)} %fusion.128, f32[12,512,512]{1,2,0:T(8,128)} %copy-done.1, ...), kind=kOutput, calls=%fused_computation.2 | convolution fusion | flops 434098176 | bytes 52502528 | tf_op jit(solution)/shard_map/qhd,khd->hqk/dot_general | solution.py:221
  244.7 23.5 %multiply_convert_fusion = (bf16[12,512,512]{1,2,0:T(8,128)(2,1)}, bf16[12,512,512]{1,2,0:T(8,128)(2,1)}) fusion(f32[12,512,512]{1,2,0:T(8,128)} %get-tuple-element.91, f32[12,512,512]{1,2,0:T(8,128)} %copy-done.2, f32[12,512]{1,0:T(8,128)S(1)} %add.316, f32[12,512]{1,0:T(8,128)} %copy-done.36, pred[512,512]{0,1:T(8,128)(4,1)} %get-tuple-element.76, ...), kind=kLoop, calls=%fused_computation | loop fusion | flops 37748736 | bytes 63488000 | tf_op jit(solution)/shard_map/convert_element_type | solution.py:228
  268.2 4.1 fusion.130
  283.3 13.0 collective-permute-done.4
  297.4 4.1 convolution_convert_fusion.2
  301.6 332.4 %all-reduce.21.cloned.1.call-done = (bf16[768,2304]{1,0:T(8,128)(2,1)}, bf16[768,768]{1,0:T(8,128)(2,1)}, bf16[768,3072]{1,0:T(8,128)(2,1)}, bf16[3072,768]{1,0:T(8,128)(2,1)}) async-done(((bf16[768,2304]{1,0:T(8,128)(2,1)}, bf16[768,768]{1,0:T(8,128)(2,1)}, bf16[768,3072]{1,0:T(8,128)(2,1)}, bf16[3072,768]{1,0:T(8,128)(2,1)}), (bf16[768,2304]{1,0:T(8,128)(2,1)}, bf16[768,768]{1,0:T(8,128)(2,1)}, ...) | async-done | bytes 14155792 | tf_op jit(solution)/shard_map/psum | solution.py:279
  634.1 6.8 convert_element_type.287
  643.9 5.5 convert_element_type.265
  649.3 4.9 convert_element_type.283
  654.2 201.2 %fusion.116 = (f32[16,2304]{1,0:T(8,128)}, f32[16,768]{1,0:T(8,128)}, f32[16,3072]{1,0:T(8,128)}) fusion(f32[768,2304]{1,0:T(8,128)} %convert_element_type.265, f32[768,768]{1,0:T(8,128)} %convert_element_type.272, f32[768,3072]{1,0:T(8,128)} %convert_element_type.283), kind=kCustom, calls=%all-reduce-scatter.3 | all-reduce-scatter fusion | flops 6291457 | bytes 19268096
  860.0 4.6 collective-permute-start.37
  870.3 6.1 collective-permute-start.31
  876.4 4.4 collective-permute-start.30
  883.4 5.6 collective-permute-start.28
  893.1 4.6 collective-permute-start.25
  913.3 22.8 %multiply_convert_fusion.6 = bf16[512,768]{1,0:T(8,128)(2,1)} fusion(f32[512,768]{1,0:T(8,128)} %get-tuple-element.18, bf16[3072,768]{1,0:T(8,128)(2,1)} %param.29, bf16[768,3072]{1,0:T(8,128)(2,1)} %param.27, f32[3072]{0:T(1024)S(1)} %copy-done.55, f32[512]{0:T(512)} %copy-done.58, f32[768]{0:T(1024)} %param.30, f32[768]{0:T(1024)} %param.26, ...), kind=kOutput, calls=%fused_computation.95 | convolution fusion | flops 4939186176 | bytes 11824128 | tf_op jit(solution)/shard_map/dot_general | solution.py:152
  947.0 4.8 fusion.115
  957.8 6.1 collective-permute-start.11
  966.3 4.8 collective-permute-start.9
  972.4 4.0 collective-permute-start.7
  976.4 4.0 collective-permute-start.6
  980.4 6.0 collective-permute-start.53
  987.9 6.8 collective-permute-start.52
  1008.8 11.8 collective-permute-start.45
  1020.6 4.9 collective-permute-start.44
  1025.6 7.8 collective-permute-start.43
  1035.2 10.0 all-reduce.16
  1045.2 275.1 %all-reduce.15 = (f32[768]{0:T(1024)}, f32[768]{0:T(1024)}, f32[768]{0:T(1024)}, f32[768]{0:T(1024)}, f32[768]{0:T(1024)}, /*index=5*/f32[768]{0:T(1024)}, f32[768]{0:T(1024)S(1)}, f32[3072]{0:T(1024)}, f32[768]{0:T(1024)S(1)}) all-reduce(bf16[768]{0:T(1024)(128)(2,1)} %get-tuple-element.43, ...), channel_id=3, replica_groups=mesh['seq'=2,'dp'=64] {'dp'}, use_global_device_ids=true, to_apply=%region_25.26.clone | all-reduce | flops 9216 | bytes 55296
  1330.3 25.0 %concatenate.5 = f32[268,768]{1,0:T(8,128)} concatenate(f32[12,768]{1,0:T(8,128)} %collective-permute-done.37, f32[16,768]{1,0:T(8,128)} %collective-permute-done.36, f32[16,768]{1,0:T(8,128)} %collective-permute-done.35, f32[16,768]{1,0:T(8,128)} %collective-permute-done.34, f32[16,768]{1,0:T(8,128)} %collective-permute-done.33, f32[16,768]{1,0:T(8,128)} %collective-permute-done.32, ...), dimensions={0} | concatenate | bytes 1646592
  1356.8 29.0 %concatenate.4 = f32[268,2304]{1,0:T(8,128)} concatenate(f32[12,2304]{1,0:T(8,128)} %collective-permute-done.21, f32[16,2304]{1,0:T(8,128)} %collective-permute-done.20, f32[16,2304]{1,0:T(8,128)} %copy-done.40, f32[16,2304]{1,0:T(8,128)} %copy-done.41, f32[16,2304]{1,0:T(8,128)} %copy-done.42, f32[16,2304]{1,0:T(8,128)} %copy-done.43, f32[16,2304]{1,0:T(8,128)} %copy-done.44, ...), dimensions={0} | concatenate | bytes 4939776
  1400.6 43.8 %concatenate.6 = f32[268,3072]{1,0:T(8,128)} concatenate(f32[12,3072]{1,0:T(8,128)} %copy-done.39, f32[16,3072]{1,0:T(8,128)} %collective-permute-done.52, f32[16,3072]{1,0:T(8,128)} %collective-permute-done.51, f32[16,3072]{1,0:T(8,128)} %collective-permute-done.50, f32[16,3072]{1,0:T(8,128)} %collective-permute-done.49, f32[16,3072]{1,0:T(8,128)} %collective-permute-done.48, ...), dimensions={0} | concatenate | bytes 6586368
  (383 shorter events, 197.5 us)
Async XLA Ops:
  7.2 626.9 %all-reduce.21.cloned.1.call-start = ((), (), s32[]{:S(2)}) async-start(), calls=%async_computation.2 | async-start | bytes 28311552 | tf_op jit(solution)/shard_map/psum | solution.py:279
  15.6 56.7 %collective-permute-start.1 = (bf16[512,768]{1,0:T(8,128)(2,1)}, bf16[512,768]{1,0:T(8,128)(2,1)}, u32[]{:S(2)}, u32[]{:S(2)}) collective-permute-start(bf16[512,768]{1,0:T(8,128)(2,1)} %get-tuple-element.71), channel_id=1, source_target_pairs={{0,64},{64,0},{1,65},{65,1},{2,66},{66,2},{3,67},{67,3},{4,68},{68... | collective-permute-start | bytes 2359304 | tf_op jit(solution)/shard_map/ppermute | solution.py:19
  19.9 33.8 %collective-permute-start = (bf16[512,768]{1,0:T(8,128)(2,1)}, bf16[512,768]{1,0:T(8,128)(2,1)}, u32[]{:S(2)}, u32[]{:S(2)}) collective-permute-start(bf16[512,768]{1,0:T(8,128)(2,1)} %slice.64), channel_id=1, source_target_pairs={{0,64},{64,0},{1,65},{65,1},{2,66},{66,2},{3,67},{67,3},{4,68},{68... | collective-permute-start | bytes 2359304 | tf_op jit(solution)/shard_map/ppermute | solution.py:19
  97.5 113.5 %collective-permute-start.3 = (bf16[512,768]{1,0:T(8,128)(2,1)}, bf16[512,768]{1,0:T(8,128)(2,1)}, u32[]{:S(2)}, u32[]{:S(2)}) collective-permute-start(bf16[512,768]{1,0:T(8,128)(2,1)} %get-tuple-element.68), channel_id=1, source_target_pairs={{0,64},{64,0},{1,65},{65,1},{2,66},{66,2},{3,67},{67,3},{4,68},{68... | collective-permute-start | bytes 2359304 | tf_op jit(solution)/shard_map/ppermute | solution.py:19
  103.2 94.2 %collective-permute-start.2 = (bf16[512,768]{1,0:T(8,128)(2,1)}, bf16[512,768]{1,0:T(8,128)(2,1)}, u32[]{:S(2)}, u32[]{:S(2)}) collective-permute-start(bf16[512,768]{1,0:T(8,128)(2,1)} %slice.63), channel_id=1, source_target_pairs={{0,64},{64,0},{1,65},{65,1},{2,66},{66,2},{3,67},{67,3},{4,68},{68... | collective-permute-start | bytes 2359304 | tf_op jit(solution)/shard_map/ppermute | solution.py:19
  207.8 73.5 %collective-permute-start.5 = (bf16[512,768]{0,1:T(8,128)(2,1)}, bf16[512,768]{0,1:T(8,128)(2,1)}, u32[]{:S(2)}, u32[]{:S(2)}) collective-permute-start(bf16[512,768]{0,1:T(8,128)(2,1)} %bitcast.26), channel_id=1, source_target_pairs={{0,64},{64,0},{1,65},{65,1},{2,66},{66,2},{3,67},{67,3},{4,68},{68... | collective-permute-start | bytes 2359304 | tf_op jit(solution)/shard_map/ppermute | solution.py:19
  276.8 19.4 %collective-permute-start.4 = (bf16[512,768]{0,1:T(8,128)(2,1)S(1)}, bf16[512,768]{0,1:T(8,128)(2,1)S(1)}, u32[]{:S(2)}, u32[]{:S(2)}) collective-permute-start(bf16[512,768]{0,1:T(8,128)(2,1)S(1)} %bitcast.123), channel_id=1, source_target_pairs={{0,64},{64,0},{1,65},{65,1},{2,66},{66,2},{3,67},{67,3},{4,68},{68... | collective-permute-start | bytes 2359304 | tf_op jit(solution)/shard_map/ppermute | solution.py:19
  301.6 1144.4 %reduce-scatter.8.cloned.1.call-start = ((), (), s32[]{:S(2)}) async-start(), calls=%async_computation.1 | async-start | bytes 9584640 | tf_op jit(solution)/shard_map/reduce_scatter | solution.py:197
  855.4 14.9 %collective-permute-start.36 = (f32[16,768]{1,0:T(8,128)}, f32[16,768]{1,0:T(8,128)}, u32[]{:S(2)}, u32[]{:S(2)}) collective-permute-start(f32[16,768]{1,0:T(8,128)} %get-tuple-element.60), channel_id=1, source_target_pairs={{0,15},{1,16},{2,17},{3,18},{4,19},{5,20},{6,21},{7,22},{8,23},{9,... | collective-permute-start | bytes 147464
  857.3 19.1 %collective-permute-start.35 = (f32[16,768]{1,0:T(8,128)}, f32[16,768]{1,0:T(8,128)}, u32[]{:S(2)}, u32[]{:S(2)}) collective-permute-start(f32[16,768]{1,0:T(8,128)} %get-tuple-element.60), channel_id=1, source_target_pairs={{0,14},{1,15},{2,16},{3,17},{4,18},{5,19},{6,20},{7,21},{8,22},{9,... | collective-permute-start | bytes 147464
  864.6 16.2 %collective-permute-start.34 = (f32[16,768]{1,0:T(8,128)}, f32[16,768]{1,0:T(8,128)}, u32[]{:S(2)}, u32[]{:S(2)}) collective-permute-start(f32[16,768]{1,0:T(8,128)} %get-tuple-element.60), channel_id=1, source_target_pairs={{0,13},{1,14},{2,15},{3,16},{4,17},{5,18},{6,19},{7,20},{8,21},{9,... | collective-permute-start | bytes 147464
  866.5 16.9 %collective-permute-start.33 = (f32[16,768]{1,0:T(8,128)}, f32[16,768]{1,0:T(8,128)}, u32[]{:S(2)}, u32[]{:S(2)}) collective-permute-start(f32[16,768]{1,0:T(8,128)} %get-tuple-element.60), channel_id=1, source_target_pairs={{0,12},{1,13},{2,14},{3,15},{4,16},{5,17},{6,18},{7,19},{8,20},{9,... | collective-permute-start | bytes 147464
  868.4 20.5 %collective-permute-start.32 = (f32[16,768]{1,0:T(8,128)}, f32[16,768]{1,0:T(8,128)}, u32[]{:S(2)}, u32[]{:S(2)}) collective-permute-start(f32[16,768]{1,0:T(8,128)} %get-tuple-element.60), channel_id=1, source_target_pairs={{0,11},{1,12},{2,13},{3,14},{4,15},{5,16},{6,17},{7,18},{8,19},{9,... | collective-permute-start | bytes 147464
  870.3 20.9 %collective-permute-start.31 = (f32[16,768]{1,0:T(8,128)}, f32[16,768]{1,0:T(8,128)}, u32[]{:S(2)}, u32[]{:S(2)}) collective-permute-start(f32[16,768]{1,0:T(8,128)} %get-tuple-element.60), channel_id=1, source_target_pairs={{0,10},{1,11},{2,12},{3,13},{4,14},{5,15},{6,16},{7,17},{8,18},{9,... | collective-permute-start | bytes 147464
  876.4 16.7 %collective-permute-start.30 = (f32[16,768]{1,0:T(8,128)}, f32[16,768]{1,0:T(8,128)}, u32[]{:S(2)}, u32[]{:S(2)}) collective-permute-start(f32[16,768]{1,0:T(8,128)} %get-tuple-element.60), channel_id=1, source_target_pairs={{0,9},{1,10},{2,11},{3,12},{4,13},{5,14},{6,15},{7,16},{8,17},{9,1... | collective-permute-start | bytes 147464
  880.9 21.0 %collective-permute-start.29 = (f32[16,768]{1,0:T(8,128)}, f32[16,768]{1,0:T(8,128)}, u32[]{:S(2)}, u32[]{:S(2)}) collective-permute-start(f32[16,768]{1,0:T(8,128)} %get-tuple-element.60), channel_id=1, source_target_pairs={{0,8},{1,9},{2,10},{3,11},{4,12},{5,13},{6,14},{7,15},{8,16},{9,17... | collective-permute-start | bytes 147464
  883.4 20.4 %collective-permute-start.28 = (f32[16,768]{1,0:T(8,128)}, f32[16,768]{1,0:T(8,128)}, u32[]{:S(2)}, u32[]{:S(2)}) collective-permute-start(f32[16,768]{1,0:T(8,128)} %get-tuple-element.60), channel_id=1, source_target_pairs={{0,7},{1,8},{2,9},{3,10},{4,11},{5,12},{6,13},{7,14},{8,15},{9,16}... | collective-permute-start | bytes 147464
  889.0 16.7 %collective-permute-start.27 = (f32[16,768]{1,0:T(8,128)}, f32[16,768]{1,0:T(8,128)}, u32[]{:S(2)}, u32[]{:S(2)}) collective-permute-start(f32[16,768]{1,0:T(8,128)} %get-tuple-element.60), channel_id=1, source_target_pairs={{0,6},{1,7},{2,8},{3,9},{4,10},{5,11},{6,12},{7,13},{8,14},{9,15},... | collective-permute-start | bytes 147464
  891.2 17.4 %collective-permute-start.26 = (f32[16,768]{1,0:T(8,128)}, f32[16,768]{1,0:T(8,128)}, u32[]{:S(2)}, u32[]{:S(2)}) collective-permute-start(f32[16,768]{1,0:T(8,128)} %get-tuple-element.60), channel_id=1, source_target_pairs={{0,5},{1,6},{2,7},{3,8},{4,9},{5,10},{6,11},{7,12},{8,13},{9,14},{... | collective-permute-start | bytes 147464
  893.1 17.9 %collective-permute-start.25 = (f32[16,768]{1,0:T(8,128)}, f32[16,768]{1,0:T(8,128)}, u32[]{:S(2)}, u32[]{:S(2)}) collective-permute-start(f32[16,768]{1,0:T(8,128)} %get-tuple-element.60), channel_id=1, source_target_pairs={{0,4},{1,5},{2,6},{3,7},{4,8},{5,9},{6,10},{7,11},{8,12},{9,13},{1... | collective-permute-start | bytes 147464
  901.9 35.1 %collective-permute-start.24 = (f32[16,768]{1,0:T(8,128)}, f32[16,768]{1,0:T(8,128)}, u32[]{:S(2)}, u32[]{:S(2)}) collective-permute-start(f32[16,768]{1,0:T(8,128)} %get-tuple-element.60), channel_id=1, source_target_pairs={{0,3},{1,4},{2,5},{3,6},{4,7},{5,8},{6,9},{7,10},{8,11},{9,12},{10... | collective-permute-start | bytes 147464
  903.8 35.1 %collective-permute-start.23 = (f32[16,768]{1,0:T(8,128)}, f32[16,768]{1,0:T(8,128)}, u32[]{:S(2)}, u32[]{:S(2)}) collective-permute-start(f32[16,768]{1,0:T(8,128)} %get-tuple-element.60), channel_id=1, source_target_pairs={{0,2},{1,3},{2,4},{3,5},{4,6},{5,7},{6,8},{7,9},{8,10},{9,11},{10,... | collective-permute-start | bytes 147464
  905.7 34.7 %collective-permute-start.22 = (f32[16,768]{1,0:T(8,128)}, f32[16,768]{1,0:T(8,128)}, u32[]{:S(2)}, u32[]{:S(2)}) collective-permute-start(f32[16,768]{1,0:T(8,128)} %get-tuple-element.60), channel_id=1, source_target_pairs={{0,1},{1,2},{2,3},{3,4},{4,5},{5,6},{6,7},{7,8},{8,9},{9,10},{10,1... | collective-permute-start | bytes 147464
  908.6 35.9 %collective-permute-start.20 = (f32[16,2304]{1,0:T(8,128)}, f32[16,2304]{1,0:T(8,128)}, u32[]{:S(2)}, u32[]{:S(2)}) collective-permute-start(f32[16,2304]{1,0:T(8,128)} %get-tuple-element.59), channel_id=1, source_target_pairs={{0,15},{1,16},{2,17},{3,18},{4,19},{5,20},{6,21},{7,22},{8,23},{9,... | collective-permute-start | bytes 442376
  911.0 31.6 %collective-permute-start.21 = (f32[12,2304]{1,0:T(8,128)}, f32[12,2304]{1,0:T(8,128)}, u32[]{:S(2)}, u32[]{:S(2)}) collective-permute-start(f32[12,2304]{1,0:T(8,128)} %slice.46), channel_id=1, source_target_pairs={{0,16},{1,17},{2,18},{3,19},{4,20},{5,21},{6,22},{7,23},{8,24},{9,... | collective-permute-start | bytes 331784
  936.9 14.8 %collective-permute-start.19 = (f32[16,2304]{1,0:T(8,128)}, f32[16,2304]{1,0:T(8,128)S(1)}, u32[]{:S(2)}, u32[]{:S(2)}) collective-permute-start(f32[16,2304]{1,0:T(8,128)} %get-tuple-element.59), channel_id=1, source_target_pairs={{0,14},{1,15},{2,16},{3,17},{4,18},{5,19},{6,20},{7,21},{8,22},{9,... | collective-permute-start | bytes 442376
  938.9 14.2 collective-permute-start.18
  940.4 14.3 collective-permute-start.17
  942.6 15.2 %collective-permute-start.16 = (f32[16,2304]{1,0:T(8,128)}, f32[16,2304]{1,0:T(8,128)S(1)}, u32[]{:S(2)}, u32[]{:S(2)}) collective-permute-start(f32[16,2304]{1,0:T(8,128)} %get-tuple-element.59), channel_id=1, source_target_pairs={{0,11},{1,12},{2,13},{3,14},{4,15},{5,16},{6,17},{7,18},{8,19},{9,... | collective-permute-start | bytes 442376
  944.6 19.4 %collective-permute-start.15 = (f32[16,2304]{1,0:T(8,128)}, f32[16,2304]{1,0:T(8,128)S(1)}, u32[]{:S(2)}, u32[]{:S(2)}) collective-permute-start(f32[16,2304]{1,0:T(8,128)} %get-tuple-element.59), channel_id=1, source_target_pairs={{0,10},{1,11},{2,12},{3,13},{4,14},{5,15},{6,16},{7,17},{8,18},{9,... | collective-permute-start | bytes 442376
  951.8 14.5 collective-permute-start.14
  953.1 17.9 %collective-permute-start.13 = (f32[16,2304]{1,0:T(8,128)S(1)}, f32[16,2304]{1,0:T(8,128)S(1)}, u32[]{:S(2)}, u32[]{:S(2)}) collective-permute-start(f32[16,2304]{1,0:T(8,128)S(1)} %copy-done.29), channel_id=1, source_target_pairs={{0,8},{1,9},{2,10},{3,11},{4,12},{5,13},{6,14},{7,15},{8,16},{9,17... | collective-permute-start | bytes 442376
  954.7 17.6 %collective-permute-start.12 = (f32[16,2304]{1,0:T(8,128)S(1)}, f32[16,2304]{1,0:T(8,128)S(1)}, u32[]{:S(2)}, u32[]{:S(2)}) collective-permute-start(f32[16,2304]{1,0:T(8,128)S(1)} %copy-done.29), channel_id=1, source_target_pairs={{0,7},{1,8},{2,9},{3,10},{4,11},{5,12},{6,13},{7,14},{8,15},{9,16}... | collective-permute-start | bytes 442376
  957.8 18.6 %collective-permute-start.11 = (f32[16,2304]{1,0:T(8,128)S(1)}, f32[16,2304]{1,0:T(8,128)S(1)}, u32[]{:S(2)}, u32[]{:S(2)}) collective-permute-start(f32[16,2304]{1,0:T(8,128)S(1)} %copy-done.29), channel_id=1, source_target_pairs={{0,6},{1,7},{2,8},{3,9},{4,10},{5,11},{6,12},{7,13},{8,14},{9,15},... | collective-permute-start | bytes 442376
  963.9 16.5 %collective-permute-start.10 = (f32[16,2304]{1,0:T(8,128)S(1)}, f32[16,2304]{1,0:T(8,128)S(1)}, u32[]{:S(2)}, u32[]{:S(2)}) collective-permute-start(f32[16,2304]{1,0:T(8,128)S(1)} %copy-done.29), channel_id=1, source_target_pairs={{0,5},{1,6},{2,7},{3,8},{4,9},{5,10},{6,11},{7,12},{8,13},{9,14},{... | collective-permute-start | bytes 442376
  966.3 21.6 %collective-permute-start.9 = (f32[16,2304]{1,0:T(8,128)S(1)}, f32[16,2304]{1,0:T(8,128)S(1)}, u32[]{:S(2)}, u32[]{:S(2)}) collective-permute-start(f32[16,2304]{1,0:T(8,128)S(1)} %copy-done.29), channel_id=1, source_target_pairs={{0,4},{1,5},{2,6},{3,7},{4,8},{5,9},{6,10},{7,11},{8,12},{9,13},{1... | collective-permute-start | bytes 442376
  971.0 23.7 %collective-permute-start.8 = (f32[16,2304]{1,0:T(8,128)S(1)}, f32[16,2304]{1,0:T(8,128)S(1)}, u32[]{:S(2)}, u32[]{:S(2)}) collective-permute-start(f32[16,2304]{1,0:T(8,128)S(1)} %copy-done.29), channel_id=1, source_target_pairs={{0,3},{1,4},{2,5},{3,6},{4,7},{5,8},{6,9},{7,10},{8,11},{9,12},{10... | collective-permute-start | bytes 442376
  972.4 25.8 %collective-permute-start.7 = (f32[16,2304]{1,0:T(8,128)S(1)}, f32[16,2304]{1,0:T(8,128)S(1)}, u32[]{:S(2)}, u32[]{:S(2)}) collective-permute-start(f32[16,2304]{1,0:T(8,128)S(1)} %copy-done.29), channel_id=1, source_target_pairs={{0,2},{1,3},{2,4},{3,5},{4,6},{5,7},{6,8},{7,9},{8,10},{9,11},{10,... | collective-permute-start | bytes 442376
  976.4 23.9 %collective-permute-start.6 = (f32[16,2304]{1,0:T(8,128)S(1)}, f32[16,2304]{1,0:T(8,128)S(1)}, u32[]{:S(2)}, u32[]{:S(2)}) collective-permute-start(f32[16,2304]{1,0:T(8,128)S(1)} %copy-done.29), channel_id=1, source_target_pairs={{0,1},{1,2},{2,3},{3,4},{4,5},{5,6},{6,7},{7,8},{8,9},{9,10},{10,1... | collective-permute-start | bytes 442376
  980.4 21.8 %collective-permute-start.53 = (f32[12,3072]{1,0:T(8,128)S(1)}, f32[12,3072]{1,0:T(8,128)S(1)}, u32[]{:S(2)}, u32[]{:S(2)}) collective-permute-start(f32[12,3072]{1,0:T(8,128)S(1)} %slice.48), channel_id=1, source_target_pairs={{0,16},{1,17},{2,18},{3,19},{4,20},{5,21},{6,22},{7,23},{8,24},{9,... | collective-permute-start | bytes 442376
  987.9 16.4 %collective-permute-start.52 = (f32[16,3072]{1,0:T(8,128)}, f32[16,3072]{1,0:T(8,128)}, u32[]{:S(2)}, u32[]{:S(2)}) collective-permute-start(f32[16,3072]{1,0:T(8,128)} %get-tuple-element.61), channel_id=1, source_target_pairs={{0,15},{1,16},{2,17},{3,18},{4,19},{5,20},{6,21},{7,22},{8,23},{9,... | collective-permute-start | bytes 589832
  1000.3 20.3 %collective-permute-start.49 = (f32[16,3072]{1,0:T(8,128)}, f32[16,3072]{1,0:T(8,128)}, u32[]{:S(2)}, u32[]{:S(2)}) collective-permute-start(f32[16,3072]{1,0:T(8,128)} %get-tuple-element.61), channel_id=1, source_target_pairs={{0,12},{1,13},{2,14},{3,15},{4,16},{5,17},{6,18},{7,19},{8,20},{9,... | collective-permute-start | bytes 589832
  1002.3 23.3 %collective-permute-start.48 = (f32[16,3072]{1,0:T(8,128)}, f32[16,3072]{1,0:T(8,128)}, u32[]{:S(2)}, u32[]{:S(2)}) collective-permute-start(f32[16,3072]{1,0:T(8,128)} %get-tuple-element.61), channel_id=1, source_target_pairs={{0,11},{1,12},{2,13},{3,14},{4,15},{5,16},{6,17},{7,18},{8,19},{9,... | collective-permute-start | bytes 589832
  1004.2 381.5 %collective-permute-start.47 = (f32[16,3072]{1,0:T(8,128)}, f32[16,3072]{1,0:T(8,128)}, u32[]{:S(2)}, u32[]{:S(2)}) collective-permute-start(f32[16,3072]{1,0:T(8,128)} %get-tuple-element.61), channel_id=1, source_target_pairs={{0,10},{1,11},{2,12},{3,13},{4,14},{5,15},{6,16},{7,17},{8,18},{9,... | collective-permute-start | bytes 589832
  1006.2 381.5 %collective-permute-start.46 = (f32[16,3072]{1,0:T(8,128)}, f32[16,3072]{1,0:T(8,128)}, u32[]{:S(2)}, u32[]{:S(2)}) collective-permute-start(f32[16,3072]{1,0:T(8,128)} %get-tuple-element.61), channel_id=1, source_target_pairs={{0,9},{1,10},{2,11},{3,12},{4,13},{5,14},{6,15},{7,16},{8,17},{9,1... | collective-permute-start | bytes 589832
  1008.8 380.9 %collective-permute-start.45 = (f32[16,3072]{1,0:T(8,128)}, f32[16,3072]{1,0:T(8,128)}, u32[]{:S(2)}, u32[]{:S(2)}) collective-permute-start(f32[16,3072]{1,0:T(8,128)} %get-tuple-element.61), channel_id=1, source_target_pairs={{0,8},{1,9},{2,10},{3,11},{4,12},{5,13},{6,14},{7,15},{8,16},{9,17... | collective-permute-start | bytes 589832
  1020.6 371.1 %collective-permute-start.44 = (f32[16,3072]{1,0:T(8,128)}, f32[16,3072]{1,0:T(8,128)}, u32[]{:S(2)}, u32[]{:S(2)}) collective-permute-start(f32[16,3072]{1,0:T(8,128)} %get-tuple-element.61), channel_id=1, source_target_pairs={{0,7},{1,8},{2,9},{3,10},{4,11},{5,12},{6,13},{7,14},{8,15},{9,16}... | collective-permute-start | bytes 589832
  1025.6 368.1 %collective-permute-start.43 = (f32[16,3072]{1,0:T(8,128)}, f32[16,3072]{1,0:T(8,128)}, u32[]{:S(2)}, u32[]{:S(2)}) collective-permute-start(f32[16,3072]{1,0:T(8,128)} %get-tuple-element.61), channel_id=1, source_target_pairs={{0,6},{1,7},{2,8},{3,9},{4,10},{5,11},{6,12},{7,13},{8,14},{9,15},... | collective-permute-start | bytes 589832
  (110 other events, 2323.2 us)
Sparse Core Ops, SparseCore 0:
  301.7 332.3 all-reduce.20
  641.0 307.5 reduce-scatter.7
where the time goes:
time: 1470 us; the launch traced here: 1450 us
  blocking collectives  486 us (33%)
  waiting for transfers between devices  359 us (24%)
  matrix products  189 us (13%)
  starting transfers between devices  163 us (11%)
  local copies, waits for them, and re-layouts  157 us (11%)
  other arithmetic  77.8 us (5%)
  between operations  21.5 us (1%)
    unnamed x2, blocking collectives  476 us
    psum x1, waiting for transfers between devices, body(): lax.psum(attend_terms[0].astype(jnp.bfloat16), 'seq').astype(jnp.float32)  332 us
    unnamed x48, starting transfers between devices  152 us
    unnamed x223, local copies, waits for them, and re-layouts  128 us
  transfers between devices with their start and end apart: 56, of which 5 were waited for; matrix products, arithmetic and copies ran while one was open for 39% of the time, Pallas kernels for 0%

commit v1 on v0

v1 whole, which is shorter than its diff:
```python
import jax
import jax.numpy as jnp
from jax import lax
from jax.experimental import pallas as pl
from jax.experimental.pallas import tpu as pltpu
from jax.sharding import PartitionSpec as P

F32 = jnp.float32
BF = jnp.bfloat16
EPS = 1e-06
ROWS = 512
WIDTH = 768
TILE = 256
CHUNKS = 11
SLOTS = 7
FEATURES = 37
MESH = pl.DeviceIdType.MESH


def dot_nn(left, right):
    return lax.dot_general(left, right, (((1,), (0,)), ((), ())), preferred_element_type=F32)


def dot_nt(left, right):
    return lax.dot_general(left, right, (((1,), (1,)), ((), ())), preferred_element_type=F32)


def dot_tn(left, right):
    return lax.dot_general(left, right, (((0,), (0,)), ((), ())), preferred_element_type=F32)


def norm_parts(block):
    centred = block - jnp.mean(block, axis=-1, keepdims=True)
    spread = jnp.mean(centred * centred, axis=-1, keepdims=True)
    inverse = lax.rsqrt(spread + EPS)
    return centred * inverse, inverse


def kernel(
    counts_ref,
    lengths_ref,
    tokens_hbm,
    cot_hbm,
    wi_hbm,
    wo_hbm,
    wu_hbm,
    wd_hbm,
    qb_ref,
    vb_ref,
    ob_ref,
    fg_ref,
    fs_ref,
    sg_ref,
    ss_ref,
    ub_ref,
    db_ref,
    lo_hbm,
    gt_hbm,
    gi_ref,
    gqb_ref,
    gvb_ref,
    go_ref,
    gob_ref,
    gfg_ref,
    gfs_ref,
    gsg_ref,
    gss_ref,
    gu_ref,
    gub_ref,
    gd_ref,
    gdb_ref,
    W,
    CH,
    R0,
    R1,
    R2,
    R3,
    FT,
    FDO,
    STAT,
    FSTAT,
    QO,
    KO,
    VO,
    QF,
    KF,
    VF,
    TOK,
    COT,
    ATT,
    SEC,
    ACT,
    DH,
    XT,
    RES,
    ACC1,
    ACC2,
    MF,
    PB,
    VS,
    VR,
    wsem,
    iosem,
    xsend,
    xrecv,
    rsend,
    rrecv,
    vsend,
    vrecv,
):
    part = lax.axis_index("seq")
    dp = lax.axis_index("dp")
    y_lo = dp // 32
    z = (dp // 8) % 4
    x = (dp // 2) % 4
    core = dp % 2
    y = 2 * part + y_lo

    def device(yy, zz, xx, cc):
        return (yy // 2, ((yy % 2) * 4 + zz) * 8 + xx * 2 + cc)

    sibling = device(y, z, x, 1 - core)
    z_of = [(z + k) % 4 for k in range(4)]
    x_of = [(x + k) % 4 for k in range(4)]
    y_of = [(y + k) % 4 for k in range(4)]
    z_peer = [device(y, v, x, core) for v in z_of]
    x_peer = [device(y, z, v, core) for v in x_of]
    y_peer = [device(v, z, x, core) for v in y_of]
    partner = y_peer[2]

    def load(src, dst, sem):
        copy = pltpu.make_async_copy(src, dst, sem)
        copy.start()
        return copy

    tok_load = load(tokens_hbm, TOK, iosem.at[0])
    w_load = {}
    for i in range(3):
        w_load[i] = load(wi_hbm.at[:, pl.ds(WIDTH * i, WIDTH)], W.at[i], wsem.at[i])
    cot_load = load(cot_hbm, COT, iosem.at[1])
    w_load[3] = load(wo_hbm, W.at[3], wsem.at[3])

    def load_ffn(f):
        slot = f % 2
        up = load(wu_hbm.at[:, pl.ds(WIDTH * f, WIDTH)], W.at[4 + slot], wsem.at[4 + slot])
        down = load(wd_hbm.at[pl.ds(WIDTH * f, WIDTH)], W.at[6 + slot], wsem.at[6 + slot])
        return up, down

    ffn_load = {0: load_ffn(0), 1: load_ffn(1)}

    barrier = pltpu.get_barrier_semaphore()
    for peer in [sibling] + z_peer[1:] + x_peer[1:] + y_peer[1:]:
        pl.semaphore_signal(barrier, inc=1, device_id=peer, device_id_type=MESH)
    pl.semaphore_wait(barrier, 10)

    def remote(src, dst, send, recv, peer):
        copy = pltpu.make_async_remote_copy(
            src_ref=src,
            dst_ref=dst,
            send_sem=send,
            recv_sem=recv,
            device_id=peer,
            device_id_type=MESH,
        )
        copy.start()
        return copy

    far_tokens = remote(tokens_hbm, FT, xsend.at[0], xrecv.at[0], partner)

    sent = {}

    def rs_core(c):
        sent[c, 0] = [
            remote(
                CH.at[c % SLOTS, :, :, :, 1 - core],
                R0.at[c],
                rsend.at[c, 0],
                rrecv.at[c, 0],
                sibling,
            )
        ]

    def rs_first(c):
        sent[c, 0][0].wait_recv()

        def add(i, carry):
            yl, zz = i // 4, i % 4
            R0[c, yl, zz] = (
                R0[c, yl, zz].astype(F32) + CH[c % SLOTS, yl, zz, :, core].astype(F32)
            ).astype(BF)
            return carry

        lax.fori_loop(0, 8, add, 0)
        sent[c, 1] = []
        for k in (2, 1, 3):
            if c % 2 == 0:
                src, peer = R0.at[c, :, z_of[k]], z_peer[k]
            else:
                src, peer = R0.at[c, :, :, x_of[k]], x_peer[k]
            sent[c, 1].append(
                remote(src, R1.at[c, k - 1], rsend.at[c, k], rrecv.at[c, k], peer)
            )

    def rs_second(c):
        for copy in sent[c, 1]:
            copy.wait_recv()
        for yl in range(2):
            own = R0[c, yl, z] if c % 2 == 0 else R0[c, yl, :, x]
            total = own.astype(F32)
            for k in range(3):
                total = total + R1[c, k, yl].astype(F32)
            R1[c, 0, yl] = total.astype(BF)
        sent[c, 2] = []
        for k in (2, 1, 3):
            if c % 2 == 0:
                src, peer = R1.at[c, 0, :, x_of[k]], x_peer[k]
            else:
                src, peer = R1.at[c, 0, :, z_of[k]], z_peer[k]
            sent[c, 2].append(
                remote(src, R2.at[c, k - 1], rsend.at[c, 3 + k], rrecv.at[c, 3 + k], peer)
            )

    def rs_y(c):
        for copy in sent[c, 2]:
            copy.wait_recv()
        own = R1[c, 0, :, x] if c % 2 == 0 else R1[c, 0, :, z]
        total = own.astype(F32)
        for k in range(3):
            total = total + R2[c, k].astype(F32)
        R2[c, 0] = total.astype(BF)
        sent[c, 3] = []
        for k in (2, 1, 3):
            sent[c, 3].append(
                remote(
                    R2.at[c, 0, y_of[k] % 2],
                    R3.at[c, k - 1],
                    rsend.at[c, 6 + k],
                    rrecv.at[c, 6 + k],
                    y_peer[k],
                )
            )

    def rs_end(c):
        for copy in sent[c, 3]:
            copy.wait_recv()
        total = R2[c, 0, y_lo].astype(F32)
        for k in range(3):
            total = total + R3[c, k].astype(F32)
        if c < 4:
            gu_ref[:, WIDTH * c : WIDTH * (c + 1)] = total[0:12]
        elif c < 7:
            gd_ref[16 * (c - 4) : 16 * (c - 3), :] = total
        elif c == 7:
            go_ref[...] = total[0:12]
        else:
            j = c - 8
            for b in range(3):
                gi_ref[:, WIDTH * b + TILE * j : WIDTH * b + TILE * (j + 1)] = total[
                    0:12, TILE * b : TILE * (b + 1)
                ]

    counts0 = counts_ref[0, 0]
    counts1 = counts_ref[0, 1]
    end0 = lengths_ref[0, 0]
    end1 = end0 + lengths_ref[0, 1]
    end2 = end1 + lengths_ref[0, 2]
    end3 = end2 + lengths_ref[0, 3]

    def used_rows(start, size, width):
        place = lax.broadcasted_iota(jnp.int32, (size, width), 0) + start
        return place < counts0 + part * (counts1 - counts0)

    def features(base, which):
        place = lax.broadcasted_iota(jnp.int32, (ROWS, 128), 0)
        shifted = place + which * counts0
        index = jnp.zeros((ROWS, 128), jnp.int32)
        for end in (end0, end1, end2, end3):
            index = index + jnp.where(end <= shifted, 1, 0)
        owned = counts0 + which * (counts1 - counts0)
        ids = jnp.where(place < owned, index, 4 + which * ROWS + place)
        lane = lax.broadcasted_iota(jnp.int32, (ROWS, 128), 1)
        high = lane >= 64
        spot = jnp.where(high, lane - 64, lane)
        digit = jnp.where(
            spot < 16, ids & 15, jnp.where(spot < 32, ((ids >> 4) & 15) + 16, (ids >> 8) + 32)
        )
        hot = jnp.where(digit == spot, 1.0, 0.0)
        query = jnp.where(spot < FEATURES, 1.0 - hot, 0.0)
        key = hot * -1e30
        MF[base] = jnp.where(high, query, 0.0).astype(BF)
        MF[base + 1] = jnp.where(high, 0.0, query).astype(BF)
        MF[base + 2] = jnp.where(high, key, 0.0).astype(BF)
        MF[base + 3] = jnp.where(high, 0.0, key).astype(BF)

    features(0, part)
    features(4, 1 - part)
    lane_row = lax.broadcasted_iota(jnp.int32, (1, 128), 1)
    select = [
        jnp.where(lane_row < 64, 1.0, 0.0).astype(BF),
        jnp.where(lane_row < 64, 0.0, 1.0).astype(BF),
    ]

    rho = lax.broadcasted_iota(jnp.int32, (ROWS, 384), 0)
    feature = lax.broadcasted_iota(jnp.int32, (ROWS, 384), 1)
    within = rho & 15
    PB[...] = jnp.where(
        (within < 12) & (feature == (rho >> 4) * 12 + within), 1.0, 0.0
    ).astype(BF)

    def padded_transpose(source):
        for b in range(2):
            XT[ROWS * b : ROWS * (b + 1), :] = dot_nt(
                PB[...], source[:, 384 * b : 384 * (b + 1)]
            ).astype(BF)

    def chunk_matmul(c, right):
        def block(m, carry):
            start = pl.multiple_of(m * TILE, TILE)
            out = dot_nn(XT[pl.ds(start, TILE), :], right())
            CH[c % SLOTS, m // 2, pl.ds(2 * (m % 2), 2)] = out.astype(BF).reshape(
                2, 4, 2, 16, WIDTH
            )
            return carry

        lax.fori_loop(0, 4, block, 0)

    ones = jnp.ones((16, ROWS), BF)

    def row_sum(block):
        return dot_nn(ones, block)[0:1]

    def tiles(step):
        def run(t, carry):
            step(pl.ds(pl.multiple_of(t * TILE, TILE), TILE), t * TILE)
            return carry

        lax.fori_loop(0, ROWS // TILE, run, 0)

    qb = qb_ref[...].reshape(1, WIDTH)
    vb = vb_ref[...].reshape(1, WIDTH)
    ob = ob_ref[...].reshape(1, WIDTH)
    fg = fg_ref[...].reshape(1, WIDTH)
    fs = fs_ref[...].reshape(1, WIDTH)
    sg = sg_ref[...].reshape(1, WIDTH)
    ss = ss_ref[...].reshape(1, WIDTH)
    db = db_ref[...].reshape(1, WIDTH)

    def project(source, q_ref, k_ref, v_ref):
        def step(rows, start):
            unit, _ = norm_parts(source[rows, :].astype(F32))
            normed = (unit * fg + fs).astype(BF)
            q = (dot_nn(normed, W[0]) + qb).astype(BF)
            q_ref[rows, :] = q * jnp.asarray(0.125, BF)
            k_ref[rows, :] = dot_nn(normed, W[1]).astype(BF)
            v_ref[rows, :] = (dot_nn(normed, W[2]) + vb).astype(BF)

        tiles(step)

    tok_load.wait()
    for i in range(3):
        w_load[i].wait()
    project(TOK, QO, KO, VO)

    cot_load.wait()

    def mask_cot(rows, start):
        used = used_rows(start, TILE, WIDTH)
        COT[rows, :] = jnp.where(used, COT[rows, :].astype(F32), 0.0).astype(BF)

    tiles(mask_cot)

    far_tokens.wait_recv()
    project(FT, QF, KF, VF)

    def pair_cols(hp):
        return pl.ds(pl.multiple_of(hp * 128, 128), 128)

    def attend(hp, carry):
        cols = pair_cols(hp)
        q = QO[:, cols]
        ko = KO[:, cols]
        kf = KF[:, cols]
        vo_t = VO[:, cols].T
        vf_t = VF[:, cols].T
        outs = []
        for h in range(2):
            qm = q * select[h] + MF[h]
            near = dot_nt(ko * select[h] + MF[2 + h], qm)
            far = dot_nt(kf * select[h] + MF[6 + h], qm)
            top = jnp.maximum(
                jnp.max(near, axis=0, keepdims=True), jnp.max(far, axis=0, keepdims=True)
            )
            near = jnp.exp(near - top)
            far = jnp.exp(far - top)
            total = jnp.sum(near, axis=0, keepdims=True) + jnp.sum(far, axis=0, keepdims=True)
            mixed = dot_nn(vo_t[64 * h : 64 * h + 64], near.astype(BF)) + dot_nn(
                vf_t[64 * h : 64 * h + 64], far.astype(BF)
            )
            outs.append(mixed * (1.0 / total))
            STAT[0, pl.ds(2 * hp + h, 1), :] = top + jnp.log(total)
        ATT[:, cols] = jnp.concatenate(outs, axis=0).T.astype(BF)
        return carry

    lax.fori_loop(0, 6, attend, 0)

    w_load[3].wait()

    def out_step(rows, start):
        res = TOK[rows, :].astype(F32) + dot_nn(ATT[rows, :], W[3]) + ob
        RES[rows, :] = res
        unit, _ = norm_parts(res)
        SEC[rows, :] = (unit * sg + ss).astype(BF)
        ACC1[rows, :] = jnp.zeros((TILE, WIDTH), F32)
        ACC2[rows, :] = jnp.zeros((TILE, WIDTH), F32)

    tiles(out_step)
    padded_transpose(SEC)
    VS[0] = jnp.zeros((16, WIDTH), F32)

    for f in range(4):
        slot = f % 2
        for copy in ffn_load[f]:
            copy.wait()
        ub = ub_ref[WIDTH * f : WIDTH * (f + 1)].reshape(1, WIDTH)

        def ffn_step(rows, start, slot=slot, ub=ub):
            dout = COT[rows, :]
            hidden = dot_nn(SEC[rows, :], W[4 + slot]) + ub
            cdf = 0.5 * (1.0 + lax.erf(hidden * 0.7071067811865476))
            density = jnp.exp(-0.5 * hidden * hidden) * 0.3989422804014327
            active = (hidden * cdf).astype(BF)
            ACT[rows, :] = active
            dhidden = (dot_nt(dout, W[6 + slot]) * (cdf + hidden * density)).astype(BF)
            DH[rows, :] = dhidden
            ACC1[rows, :] += dot_nn(active, W[6 + slot])
            ACC2[rows, :] += dot_nt(dhidden, W[4 + slot])

        tiles(ffn_step)
        if f + 2 < 4:
            ffn_load[f + 2] = load_ffn(f + 2)
        chunk_matmul(f, lambda: DH[...])
        rs_core(f)
        VS[0, 8 + f : 9 + f, :] = row_sum(DH[...])

        def down_step(b, carry, f=f):
            cols = pl.ds(pl.multiple_of(b * 384, 384), 384)
            out = dot_tn(ACT[:, cols], COT[...]).astype(BF).reshape(4, 2, 3, 16, WIDTH)
            for k in range(3):
                CH[4 + k, f // 2, 2 * (f % 2) + b] = out[:, :, k]
            return carry

        lax.fori_loop(0, 2, down_step, 0)
        if f >= 1:
            rs_first(f - 1)
        if f >= 2:
            rs_second(f - 2)

    for k in range(3):
        rs_core(4 + k)
    rs_first(3)
    rs_second(2)
    rs_y(0)

    def second_back(rows, start):
        res = RES[rows, :]
        used = used_rows(start, TILE, WIDTH)
        FT[rows, :] = jnp.where(used, res + ACC1[rows, :] + db, 0.0).astype(BF)
        unit, inverse = norm_parts(res)
        dsecond = ACC2[rows, :]
        VS[0, 5:6, :] += jnp.sum(dsecond * unit, axis=0, keepdims=True)
        VS[0, 6:7, :] += jnp.sum(dsecond, axis=0, keepdims=True)
        g = dsecond * sg
        through = (
            g
            - jnp.mean(g, axis=-1, keepdims=True)
            - unit * jnp.mean(g * unit, axis=-1, keepdims=True)
        ) * inverse
        dres = COT[rows, :].astype(F32) + through
        RES[rows, :] = dres
        SEC[rows, :] = dres.astype(BF)
        DH[rows, :] = dot_nt(dres.astype(BF), W[3]).astype(BF)

    tiles(second_back)
    lo_store = load(FT, lo_hbm, iosem.at[2])
    far_dout = remote(DH, FDO, xsend.at[1], xrecv.at[1], partner)
    VS[0, 7:8, :] = row_sum(COT[...])
    VS[0, 2:3, :] = row_sum(SEC[...])

    head = lax.broadcasted_iota(jnp.int32, (16, WIDTH), 0)
    column = lax.broadcasted_iota(jnp.int32, (16, WIDTH), 1)
    in_head = jnp.where((column >> 6) == head, 1.0, 0.0).astype(BF)
    product = DH[...].astype(F32) * ATT[...].astype(F32)
    rough = product.astype(BF)
    STAT[1] = dot_nt(in_head, rough) + dot_nt(in_head, (product - rough.astype(F32)).astype(BF))
    far_stats = remote(STAT, FSTAT, xsend.at[2], xrecv.at[2], partner)

    padded_transpose(ATT)
    sent[0, 0][0].wait_send()
    chunk_matmul(7, lambda: SEC[...])
    rs_core(7)
    for k in range(3):
        rs_first(4 + k)
    rs_second(3)
    rs_y(1)
    rs_end(0)

    def own_queries(hp, carry):
        cols = pair_cols(hp)
        q = QO[:, cols]
        ko = KO[:, cols]
        kf = KF[:, cols]
        vo = VO[:, cols]
        vf = VF[:, cols]
        do = DH[:, cols]
        ko_t = ko.T
        kf_t = kf.T
        dq = []
        dk = None
        for h in range(2):
            logsum = STAT[0, pl.ds(2 * hp + h, 1), :]
            delta = STAT[1, pl.ds(2 * hp + h, 1), :]
            qm = q * select[h] + MF[h]
            qs = q * select[h]
            dom = do * select[h]
            near = jnp.exp(dot_nt(ko * select[h] + MF[2 + h], qm) - logsum)
            dnear = (near * (dot_nt(vo, dom) - delta)).astype(BF)
            far = jnp.exp(dot_nt(kf * select[h] + MF[6 + h], qm) - logsum)
            dfar = (far * (dot_nt(vf, dom) - delta)).astype(BF)
            dq.append(
                dot_nn(ko_t[64 * h : 64 * h + 64], dnear)
                + dot_nn(kf_t[64 * h : 64 * h + 64], dfar)
            )
            dk_h = dot_nn(dnear, qs)
            dv_h = dot_nn(near.astype(BF), dom)
            dk, dv = (dk_h, dv_h) if dk is None else (dk + dk_h, dv + dv_h)
        ACC1[:, cols] = dk
        ACC2[:, cols] = dv
        QO[:, cols] = (jnp.concatenate(dq, axis=0).T * 0.125).astype(BF)
        return carry

    lax.fori_loop(0, 3, own_queries, 0)
    for k in range(3):
        rs_second(4 + k)
    rs_first(7)
    rs_y(2)
    rs_y(3)
    rs_end(1)
    lax.fori_loop(3, 6, own_queries, 0)
    for k in range(3):
        rs_y(4 + k)
    rs_second(7)
    rs_end(2)
    rs_end(3)

    def again(rows, start):
        unit, _ = norm_parts(TOK[rows, :].astype(F32))
        ATT[rows, :] = (unit * fg + fs).astype(BF)

    tiles(again)
    padded_transpose(ATT)

    far_dout.wait_recv()
    far_stats.wait_recv()

    def far_queries(hp, carry):
        cols = pair_cols(hp)
        q = QF[:, cols]
        ko = KO[:, cols]
        vo = VO[:, cols]
        do = FDO[:, cols]
        dk = ACC1[:, cols]
        dv = ACC2[:, cols]
        for h in range(2):
            logsum = FSTAT[0, pl.ds(2 * hp + h, 1), :]
            delta = FSTAT[1, pl.ds(2 * hp + h, 1), :]
            qs = q * select[h]
            dom = do * select[h]
            probs = jnp.exp(dot_nt(ko * select[h] + MF[2 + h], qs + MF[4 + h]) - logsum)
            dscores = (probs * (dot_nt(vo, dom) - delta)).astype(BF)
            dk = dk + dot_nn(dscores, qs)
            dv = dv + dot_nn(probs.astype(BF), dom)
        KO[:, cols] = dk.astype(BF)
        VO[:, cols] = dv.astype(BF)
        return carry

    for j in range(3):
        c = 8 + j
        lax.fori_loop(2 * j, 2 * j + 2, far_queries, 0)
        sent[c - 7, 0][0].wait_send()
        cols = slice(TILE * j, TILE * (j + 1))

        def joined(cols=cols):
            return jnp.concatenate([QO[:, cols], KO[:, cols], VO[:, cols]], axis=1)

        chunk_matmul(c, joined)
        rs_core(c)
        if j == 0:
            rs_y(7)
            for k in range(3):
                rs_end(4 + k)
        if j == 1:
            rs_first(8)
            rs_end(7)
        if j == 2:
            rs_first(9)
            rs_second(8)

    VS[0, 0:1, :] = row_sum(QO[...])
    VS[0, 1:2, :] = row_sum(VO[...])

    def first_back(rows, start):
        unit, inverse = norm_parts(TOK[rows, :].astype(F32))
        dnormed = (
            dot_nt(QO[rows, :], W[0]) + dot_nt(KO[rows, :], W[1]) + dot_nt(VO[rows, :], W[2])
        )
        VS[0, 3:4, :] += jnp.sum(dnormed * unit, axis=0, keepdims=True)
        VS[0, 4:5, :] += jnp.sum(dnormed, axis=0, keepdims=True)
        g = dnormed * fg
        through = (
            g
            - jnp.mean(g, axis=-1, keepdims=True)
            - unit * jnp.mean(g * unit, axis=-1, keepdims=True)
        ) * inverse
        TOK[rows, :] = (RES[rows, :] + through).astype(BF)

    far_tokens.wait_send()
    tiles(first_back)
    gt_store = load(TOK, gt_hbm, iosem.at[3])

    vsent = []

    def vec_send(step, peers, base):
        vsent.append(
            [
                remote(VS.at[step], VR.at[base + i], vsend.at[base + i], vrecv.at[base + i], peer)
                for i, peer in enumerate(peers)
            ]
        )

    def vec_add(step, base):
        total = VS[step]
        for i, copy in enumerate(vsent[step]):
            copy.wait_recv()
            total = total + VR[base + i]
        VS[step + 1] = total

    vec_send(0, [sibling], 0)
    rs_first(10)
    rs_second(9)
    rs_y(8)
    vec_add(0, 0)
    vec_send(1, z_peer[1:], 1)
    rs_second(10)
    rs_y(9)
    rs_end(8)
    vec_add(1, 1)
    vec_send(2, x_peer[1:], 4)
    rs_y(10)
    rs_end(9)
    vec_add(2, 4)
    vec_send(3, y_peer[1:], 7)
    rs_end(10)
    vec_add(3, 7)

    spot = lax.broadcasted_iota(jnp.int32, (WIDTH, 128), 0)
    lane = lax.broadcasted_iota(jnp.int32, (WIDTH, 128), 1)
    narrow = jnp.where((lane < 12) & (spot == lane + 12 * dp), 1.0, 0.0)
    wide = jnp.where((lane < 48) & (spot == lane + 48 * (dp % 16)), 1.0, 0.0)
    vectors = VS[4]
    exact = dict(precision=lax.Precision.HIGHEST, preferred_element_type=F32)
    small = jnp.dot(vectors, narrow, **exact)
    large = jnp.dot(vectors, wide, **exact)
    row = lax.broadcasted_iota(jnp.int32, (16, 128), 0)
    large = jnp.sum(jnp.where(row == 8 + dp // 16, large, 0.0), axis=0, keepdims=True)
    for i, ref in enumerate(
        (gqb_ref, gvb_ref, gob_ref, gfg_ref, gfs_ref, gsg_ref, gss_ref, gdb_ref)
    ):
        ref[...] = small[i : i + 1, 0:12].reshape(12)
    gub_ref[...] = large[:, 0:48].reshape(48)

    far_dout.wait_send()
    far_stats.wait_send()
    for c in range(CHUNKS):
        if not (c == 0 or 1 <= c <= 3):
            sent[c, 0][0].wait_send()
        for s in (1, 2, 3):
            for copy in sent[c, s]:
                copy.wait_send()
    for copies in vsent:
        for copy in copies:
            copy.wait_send()
    lo_store.wait()
    gt_store.wait()


def body(
    tokens,
    input_weight,
    query_bias,
    value_bias,
    out_weight,
    out_bias,
    first_gain,
    first_shift,
    second_gain,
    second_shift,
    up_weight,
    up_bias,
    down_weight,
    down_bias,
    cotangent,
    row_counts,
    image_lengths,
):
    hbm = pl.BlockSpec(memory_space=pl.ANY)
    vmem = pl.BlockSpec(memory_space=pltpu.VMEM)
    smem = pl.BlockSpec(memory_space=pltpu.SMEM)
    rows = jax.ShapeDtypeStruct((ROWS, WIDTH), BF)

    def f32(*shape):
        return jax.ShapeDtypeStruct(shape, F32)

    def block(kind, *lead):
        return pltpu.VMEM((*lead, ROWS, WIDTH), kind)

    out = pl.pallas_call(
        kernel,
        out_shape=(
            rows,
            rows,
            f32(12, 3 * WIDTH),
            f32(12),
            f32(12),
            f32(12, WIDTH),
            f32(12),
            f32(12),
            f32(12),
            f32(12),
            f32(12),
            f32(12, 4 * WIDTH),
            f32(48),
            f32(48, WIDTH),
            f32(12),
        ),
        in_specs=[smem, smem] + [hbm] * 6 + [vmem] * 9,
        out_specs=(hbm, hbm) + (vmem,) * 13,
        scratch_shapes=[
            pltpu.VMEM((8, WIDTH, WIDTH), BF),
            pltpu.VMEM((SLOTS, 2, 4, 4, 2, 16, WIDTH), BF),
            pltpu.VMEM((CHUNKS, 2, 4, 4, 16, WIDTH), BF),
            pltpu.VMEM((CHUNKS, 3, 2, 4, 16, WIDTH), BF),
            pltpu.VMEM((CHUNKS, 3, 2, 16, WIDTH), BF),
            pltpu.VMEM((CHUNKS, 3, 16, WIDTH), BF),
            block(BF),
            block(BF),
            pltpu.VMEM((2, 16, ROWS), F32),
            pltpu.VMEM((2, 16, ROWS), F32),
        ]
        + [block(BF)] * 12
        + [
            pltpu.VMEM((1024, ROWS), BF),
            block(F32),
            block(F32),
            block(F32),
            pltpu.VMEM((8, ROWS, 128), BF),
            pltpu.VMEM((ROWS, 384), BF),
            pltpu.VMEM((5, 16, WIDTH), F32),
            pltpu.VMEM((10, 16, WIDTH), F32),
            pltpu.SemaphoreType.DMA((8,)),
            pltpu.SemaphoreType.DMA((4,)),
            pltpu.SemaphoreType.DMA((3,)),
            pltpu.SemaphoreType.DMA((3,)),
            pltpu.SemaphoreType.DMA((CHUNKS, 10)),
            pltpu.SemaphoreType.DMA((CHUNKS, 10)),
            pltpu.SemaphoreType.DMA((10,)),
            pltpu.SemaphoreType.DMA((10,)),
        ],
        compiler_params=pltpu.CompilerParams(
            collective_id=0, has_side_effects=True, vmem_limit_bytes=61 * 2**20
        ),
        name="encoder",
    )(
        row_counts,
        image_lengths,
        tokens,
        cotangent,
        input_weight,
        out_weight,
        up_weight,
        down_weight,
        query_bias,
        value_bias,
        out_bias,
        first_gain,
        first_shift,
        second_gain,
        second_shift,
        up_bias,
        down_bias,
    )
    return out


def solution(mesh):
    rows = P(("seq", "dp"), None)
    split = P("dp", None)
    line = P("dp")
    return jax.shard_map(
        body,
        mesh=mesh,
        in_specs=(rows,) + (P(),) * 13 + (rows, split, split),
        out_specs=(
            rows,
            rows,
            split,
            line,
            line,
            split,
            line,
            line,
            line,
            line,
            line,
            split,
            line,
            split,
            line,
        ),
        check_vma=False,
    )
```

time: 1470 us -> 191 us (0.13); the launches traced: 1450 us -> 191 us
  blocking collectives: 486 us -> 0 us
  waiting for transfers between devices: 359 us -> 0 us
  matrix products: 189 us -> 0 us
  Pallas kernels: 0 us -> 170 us
  starting transfers between devices: 163 us -> 0 us
  local copies, waits for them, and re-layouts: 157 us -> 20.6 us
  other arithmetic: 77.8 us -> 0 us
  between operations: 21.5 us -> 0.67 us
    unnamed x2 -> x0, blocking collectives: 476 us -> none
    psum x1 -> x0, waiting for transfers between devices: 332 us -> none  [body(): lax.psum(attend_terms[0].astype(jnp.bfloat16), 'seq').astype(jnp.float32)]
    dot_general x29 -> x0, matrix products: 189 us -> none  [the longest x4 25.9 us: back_dot(): lax.dot_general(left, right, (((1,), (1,)), ((), ())), preferred_element_...]
    pallas_call x0 -> x1, Pallas kernels: none -> 170 us  [body(): pl.pallas_call(kernel, out_shape=(rows, rows, f32(12, 3 * WIDTH), f32(12)...]
    unnamed x48 -> x0, starting transfers between devices: 152 us -> none
    unnamed x223 -> x15, local copies, waits for them, and re-layouts: 128 us -> 20.6 us
    convert_element_type x10 -> x0, other arithmetic: 49.1 us -> none  [the longest x1 23.5 us: body(): (far_probs * (far_dprobs - delta_rows[..., None])).astype(jnp.bfloat16)]
    reduce_sum x14 -> x0, other arithmetic: 24.1 us -> none  [the longest x4 6.59 us: norm_rows(): spread = jnp.mean(centred * centred, axis=-1, keepdims=True)]
  transfers between devices with their start and end apart: 56 -> 0, of which waited for: 5 -> 0; matrix products, arithmetic and copies ran while one was open for 39% -> 0% of each run, Pallas kernels for 0% -> 0%
where the time goes in v1:
time: 191 us
  Pallas kernels  170 us (89%)
  local copies, waits for them, and re-layouts  20.6 us (11%)
    pallas_call x1, Pallas kernels, body(): pl.pallas_call(kernel, out_shape=(rows, rows, f32(12, 3 * WIDTH), f32(12)...  170 us
    unnamed x15, local copies, waits for them, and re-layouts  20.6 us

profile of v1, /device:TPU:0, one launch (start us, length us, event | category | flops | bytes accessed | tf_op | source)
XLA Modules:
  0.0 190.9 jit_solution(2240550420195240896)
XLA Ops:
  0.7 169.7 %encoder.1 = (bf16[512,768]{1,0:T(8,128)(2,1)}, bf16[512,768]{1,0:T(8,128)(2,1)}, f32[12,2304]{1,0:T(8,128)}, f32[12]{0:T(128)}, f32[12]{0:T(128)}, /*index=5*/f...) custom-call(s32[1,2]{1,0:T(1,128)} %counts_ref.1, ...), custom_call_target="tpu_custom_call" | custom-call | tf_op jit(solution)/shard_map/encoder/pallas_call | solution.py:726
  170.3 2.1 %copy.47 = bf16[512,768]{1,0:T(8,128)(2,1)} copy(bf16[512,768]{1,0:T(8,128)(2,1)} %get-tuple-element.30) | data formatting | bytes 1572864
  172.4 2.1 %copy.48 = bf16[512,768]{1,0:T(8,128)(2,1)} copy(bf16[512,768]{1,0:T(8,128)(2,1)} %get-tuple-element.31) | data formatting | bytes 1572864
  174.4 1.6 copy.49
  176.0 1.1 copy.50
  177.1 1.1 copy.51
  178.2 1.4 copy.52
  179.6 1.2 copy.53
  180.8 1.1 copy.54
  181.9 1.1 copy.55
  183.0 1.2 copy.56
  184.2 1.2 copy.57
  185.4 1.6 copy.58
  187.0 1.2 copy.59
  188.2 1.6 copy.60
  189.8 1.2 copy.61
